TPU v7x, 32 devices: a whole 2x2x4 slice. The times are simulated.
32 devices in a mesh: groups: 2 (over y), pool: 16 (over z, x, core), sub: 1.
Axes of the slice: x: 2, y: 2, z: 4, core: 2. Of those that a mesh axis runs over, the one named last changes fastest.
Arguments:
- query: bfloat16 [256, 8192], P(('groups', 'pool'), 'sub'), parts along dimension 0, may hold values from -5.5 to 5.5
- new_kv: bfloat16 [256, 2, 512], P(('groups', 'pool'), None, 'sub'), parts along dimension 0, may hold values from -5.5 to 5.5
- kv_cache: bfloat16 [256, 128, 2, 512], P(('groups', 'pool'), None, None, 'sub'), parts along dimension 0, may hold values from -5.5 to 5.5
- lengths: int32 [256], P(('groups', 'pool')), parts along dimension 0, may hold values from 1 to 128, 4096 in all
- o_weight: bfloat16 [4096, 8192], P('pool', 'sub'), may hold values from -0.25 to 0.25
- residual: bfloat16 [256, 4096], P(('groups', 'pool', 'sub')), parts along dimension 0, may hold values from -72 to 72
- norm_gain: bfloat16 [4096], replicated, may hold values from 0.099609375 to 1.8984375
- router_weight: bfloat16 [16, 4096], replicated, may hold values from -0.032470703 to 0.032470703
- expert_ids: int32 [256, 8], P(('groups', 'pool', 'sub')), parts along dimension 0, may hold values from 0 to 15, all different within a row; in each aligned block of 8 rows (0 to 7, 8 to 15, ...) at most 8 rows name the same one
- gate_weight: bfloat16 [16, 4096, 768], P('pool', None, 'sub'), may hold values from -0.078125 to 0.078125
- up_weight: bfloat16 [16, 4096, 768], P('pool', None, 'sub'), may hold values from -0.078125 to 0.078125
- down_weight: bfloat16 [16, 768, 4096], P('pool', 'sub'), may hold values from -0.29228357 to 0.29228357
Outputs:
- mixed: bfloat16 [256, 4096], P(('groups', 'pool', 'sub')), parts along dimension 0
There are 2 independent parts, one for each index of `groups`. A program takes and returns all parts, laid end to end along the dimension named above; an argument that names none is the same for every part. Nothing has to cross between parts.
Inputs may be any that keep to these rules, and one draw needn't show every extreme that they name: `expert_ids`: each row names 8 different experts. Within the 8 rows of one device (aligned blocks) no expert is named more than 8 times, a bound that some block reaches. A row attends to its cache positions below its length and to its own new key; the longest row has exactly 128. The lengths of the 128 rows of each serving group sum to 4096; the whole array, over all groups, sums to that times the number of groups.
All inputs are finite; a program needn't handle non-finite values.
Results may differ from a plain program's by a relative error of at most 0.03.
Values may be sent and summed in bfloat16 or wider, within the bound.
A program may use at most 64 MiB of HBM per device.

v0:
```python
import jax
import jax.numpy as jnp
from jax import lax
from jax.sharding import PartitionSpec as P

QH = 64
KVH = 4
HEAD = 128
TOPK = 8


norm_eps = 1e-06


def attend(query, new_kv, kv_cache, lengths):
    rows_att = query.shape[0]
    cache_len = kv_cache.shape[1]
    groups = kv_cache.shape[3] // HEAD
    per_group = QH // KVH
    queries = query.reshape(rows_att, groups, per_group, HEAD)
    cached_keys = kv_cache[:, :, 0].reshape(rows_att, cache_len, groups, HEAD)
    cached_values = kv_cache[:, :, 1].reshape(rows_att, cache_len, groups, HEAD)
    new_key = new_kv[:, 0].reshape(rows_att, groups, HEAD)
    new_value = new_kv[:, 1].reshape(rows_att, groups, HEAD)
    score_scale = HEAD ** (-0.5)
    scores = (
        jnp.einsum("rgqd,rjgd->rgqj", queries, cached_keys, preferred_element_type=jnp.float32)
        * score_scale
    )
    own_score = (
        jnp.einsum("rgqd,rgd->rgq", queries, new_key, preferred_element_type=jnp.float32)
        * score_scale
    )
    visible = jnp.arange(cache_len, dtype=jnp.int32)[None, :] < lengths[:, None]
    scores = jnp.where(visible[:, None, None, :], scores, jnp.float32(-1e30))
    row_max = jnp.maximum(jnp.max(scores, axis=-1), own_score)
    weights = jnp.exp(scores - row_max[..., None])
    own_weight = jnp.exp(own_score - row_max)
    denominator = jnp.sum(weights, axis=-1) + own_weight
    attn_probs = (weights / denominator[..., None]).astype(jnp.bfloat16)
    own_prob = (own_weight / denominator).astype(jnp.bfloat16)
    attended = jnp.einsum(
        "rgqj,rjgd->rgqd", attn_probs, cached_values, preferred_element_type=jnp.float32
    )
    attended = (
        attended
        + own_prob.astype(jnp.float32)[..., None] * new_value.astype(jnp.float32)[:, :, None, :]
    )
    return attended.astype(jnp.bfloat16).reshape(rows_att, -1)


def per_device(
    query,
    new_kv,
    kv_cache,
    lengths,
    o_weight,
    residual,
    norm_gain,
    router_weight,
    expert_ids,
    gate_weight,
    up_weight,
    down_weight,
):
    pool_size = lax.axis_size("pool")
    sub_size = lax.axis_size("sub")
    rows_dev = residual.shape[0]
    width = residual.shape[1]
    col_count = o_weight.shape[0]
    experts = router_weight.shape[0]
    attended = attend(query, new_kv, kv_cache, lengths)
    partial_value = lax.dot_general(
        lax.all_gather(attended, "pool", axis=0, tiled=True),
        o_weight,
        (((1,), (1,)), ((), ())),
        preferred_element_type=jnp.float32,
    )
    exchanged = lax.all_to_all(
        partial_value.astype(jnp.bfloat16), ("pool", "sub"), split_axis=0, concat_axis=1, tiled=True
    ).astype(partial_value.dtype)
    projected = jnp.sum(
        exchanged.reshape(rows_dev, pool_size, sub_size, col_count), axis=2
    ).reshape(rows_dev, width)
    hidden = residual.astype(jnp.float32) + projected
    mean_square = jnp.mean(hidden * hidden, axis=-1, keepdims=True)
    normed = (hidden * lax.rsqrt(mean_square + norm_eps) * norm_gain.astype(jnp.float32)).astype(
        jnp.bfloat16
    )
    logits = lax.dot_general(
        normed, router_weight, (((1,), (1,)), ((), ())), preferred_element_type=jnp.float32
    )
    onehot = expert_ids[:, :, None] == jnp.arange(experts, dtype=jnp.int32)[None, None, :]
    chosen = jnp.sum(jnp.where(onehot, logits[:, None, :], 0.0), axis=2)
    raised = jnp.exp(chosen)
    route_weight = raised / jnp.sum(raised, axis=1, keepdims=True)
    weight_full = jnp.sum(jnp.where(onehot, route_weight[:, :, None], 0.0), axis=1)
    capacity = min(rows_dev, max(2, 2 * rows_dev * TOPK // pool_size))
    member = jnp.sum(onehot.astype(jnp.int32), axis=1)
    rank_in_block = jnp.cumsum(member, axis=0) - member
    slot_ids = jnp.arange(capacity, dtype=jnp.int32)
    selector = (member.T[:, None, :] == 1) & (
        rank_in_block.T[:, None, :] == slot_ids[None, :, None]
    )
    combine_coef = jnp.where(selector, weight_full.T[:, None, :], 0.0)
    selector_bf = selector.astype(jnp.bfloat16)
    sending = jnp.einsum(
        "emr,rd->emd", selector_bf, normed, preferred_element_type=jnp.float32
    ).astype(jnp.bfloat16)
    doubled = jnp.broadcast_to(sending[:, None], (experts, sub_size, capacity, width)).reshape(
        experts * sub_size, capacity, width
    )
    arrived = lax.all_to_all(doubled, ("pool", "sub"), split_axis=0, concat_axis=0, tiled=True)
    item_count = arrived.shape[-2]
    flat_rows = arrived.reshape(-1, arrived.shape[-1])
    gate_proj = jnp.dot(flat_rows, gate_weight[0], preferred_element_type=jnp.float32)
    up_proj = jnp.dot(flat_rows, up_weight[0], preferred_element_type=jnp.float32)
    inner_act = (jax.nn.silu(gate_proj) * up_proj).astype(jnp.bfloat16)
    half_out = jnp.dot(inner_act, down_weight[0], preferred_element_type=jnp.float32).astype(
        jnp.bfloat16
    )
    returned = lax.all_to_all(
        half_out.reshape(-1, item_count, half_out.shape[-1]),
        ("pool", "sub"),
        split_axis=0,
        concat_axis=0,
        tiled=True,
    )
    merged = jnp.sum(
        returned.reshape(experts, sub_size, capacity, width).astype(jnp.float32), axis=1
    )
    mixed = jnp.einsum("emr,emd->rd", combine_coef, merged, precision=lax.Precision.HIGHEST)
    return mixed.astype(jnp.bfloat16)


def solution(mesh):
    in_specs = (
        P(("groups", "pool"), "sub"),
        P(("groups", "pool"), None, "sub"),
        P(("groups", "pool"), None, None, "sub"),
        P(("groups", "pool")),
        P("pool", "sub"),
        P(("groups", "pool", "sub"), None),
        P(),
        P(),
        P(("groups", "pool", "sub"), None),
        P("pool", None, "sub"),
        P("pool", None, "sub"),
        P("pool", "sub", None),
    )
    out_specs = P(("groups", "pool", "sub"), None)
    return jax.shard_map(
        per_device, mesh=mesh, in_specs=in_specs, out_specs=out_specs, check_vma=False
    )
```

profile of v0, /device:TPU:0, one launch (start us, length us, event | category | flops | bytes accessed | tf_op | source)
XLA Modules:
  0.0 161.1 jit_solution(8218195218705610915)
XLA Ops:
  6.6 6.5 %fusion.52 = (bf16[8,128,1,512]{3,2,1,0:T(2,128)(2,1)}, bf16[8,128,1,512]{3,2,1,0:T(2,128)(2,1)S(1)}) fusion(bf16[8,128,2,512]{3,2,1,0:T(2,128)(2,1)} %param.14), kind=kLoop, calls=%fused_computation.66 | loop fusion | bytes 4194304 | tf_op jit(solution)/shard_map/slice | solution.py:21
  13.1 4.7 %copy.44 = bf16[8,128,1,512]{1,3,0,2:T(8,128)(2,1)S(1)} copy(bf16[8,128,1,512]{3,2,1,0:T(2,128)(2,1)} %get-tuple-element.5) | data formatting | bytes 2097152
  17.9 0.6 fusion.53
  18.5 0.2 fusion.38
  18.7 1.4 fusion.54
  20.1 0.3 fusion.34
  20.4 0.6 fusion.48
  21.0 1.4 copy.46
  22.5 1.5 fusion.20
  24.0 0.8 copy.60
  24.8 0.7 convert_element_type.74
  25.5 0.8 convert_reduce_fusion
  26.3 42.7 %all-gather.2.cloned.1.call-done = bf16[128,8192]{1,0:T(8,128)(2,1)} async-done(((bf16[8,8192]{1,0:T(8,128)(2,1)}), bf16[128,8192]{1,0:T(8,128)(2,1)}) %all-gather.2.cloned.1.call-update) | async-done | bytes 2097168 | tf_op jit(solution)/shard_map/all_gather | solution.py:74
  69.0 5.0 %fusion.21 = bf16[16,8,256]{2,1,0:T(8,128)(2,1)} fusion(bf16[128,8192]{1,0:T(8,128)(2,1)} %all-gather.2.cloned.1.call-done, bf16[256,8192]{1,0:T(8,128)(2,1)} %param.16), kind=kOutput, calls=%fused_computation.18 | convolution fusion | flops 536903680 | bytes 6356992 | tf_op jit(solution)/shard_map/dot_general | solution.py:73
  74.0 3.5 %all-to-all-start = ((bf16[16,8,256]{2,1,0:T(8,128)(2,1)}), bf16[16,8,256]{2,1,0:T(8,128)(2,1)S(1)}, u32[]{:S(2)}, u32[]{:S(2)}) async-start(bf16[16,8,256]{2,1,0:T(8,128)(2,1)} %fusion.21), calls=%async_computation | async-start | bytes 131072 | tf_op jit(solution)/shard_map/all_to_all | solution.py:79
  77.6 6.7 %all-to-all-done = bf16[16,8,256]{2,1,0:T(8,128)(2,1)S(1)} async-done(((bf16[16,8,256]{2,1,0:T(8,128)(2,1)}), bf16[16,8,256]{2,1,0:T(8,128)(2,1)S(1)}, u32[]{:S(2)}, u32[]{:S(2)}) %all-to-all-start) | async-done | bytes 65568 | tf_op jit(solution)/shard_map/all_to_all | solution.py:79
  84.7 0.4 convolution_convert_fusion
  85.1 27.4 %all_to_all.23 = bf16[16,8,4096]{2,1,0:T(8,128)(2,1)S(1)} all-to-all(bf16[16,8,4096]{2,1,0:T(8,128)(2,1)S(1)} %convolution_convert_fusion), channel_id=1, replica_groups=mesh['groups'=2,'pool'=16,'sub'=1] {'pool','sub'}, dimensions={0} | all-to-all | bytes 2097152 | tf_op jit(solution)/shard_map/all_to_all | solution.py:113
  112.5 3.8 %fusion.4 = f32[128,768]{1,0:T(8,128)S(1)} fusion(bf16[1,4096,768]{2,1,0:T(8,128)(2,1)} %param.21, bf16[16,8,4096]{2,1,0:T(8,128)(2,1)S(1)} %all_to_all.23), kind=kOutput, calls=%fused_computation.4 | convolution fusion | flops 805306368 | bytes 7733248 | tf_op jit(solution)/shard_map/dot_general | solution.py:116
  116.3 8.1 %fusion.9 = bf16[16,8,4096]{2,1,0:T(8,128)(2,1)} fusion(bf16[1,768,4096]{2,1,0:T(8,128)(2,1)} %param.23, bf16[1,4096,768]{2,1,0:T(8,128)(2,1)} %param.22, bf16[16,8,4096]{2,1,0:T(8,128)(2,1)S(1)} %all_to_all.23, f32[128,768]{1,0:T(8,128)S(1)} %fusion.4), kind=kOutput, calls=%fused_computation.8 | convolution fusion | flops 1611726848 | bytes 15073280 | tf_op jit(solution)/shard_map/dot_general | solution.py:119
  124.4 4.9 %all-to-all-start.2 = ((bf16[16,8,4096]{2,1,0:T(8,128)(2,1)}), bf16[16,8,4096]{2,1,0:T(8,128)(2,1)S(1)}, u32[]{:S(2)}, u32[]{:S(2)}) async-start(bf16[16,8,4096]{2,1,0:T(8,128)(2,1)} %fusion.9), calls=%async_computation.2 | async-start | bytes 2097152 | tf_op jit(solution)/shard_map/all_to_all | solution.py:122
  129.4 0.2 select_reduce_fusion.1
  129.9 22.3 %all-to-all-done.2 = bf16[16,8,4096]{2,1,0:T(8,128)(2,1)S(1)} async-done(((bf16[16,8,4096]{2,1,0:T(8,128)(2,1)}), bf16[16,8,4096]{2,1,0:T(8,128)(2,1)S(1)}, u32[]{:S(2)}, u32[]{:S(2)}) %all-to-all-start.2) | async-done | bytes 1048608 | tf_op jit(solution)/shard_map/all_to_all | solution.py:122
  152.2 2.0 %fusion.12 = bf16[8,4096]{1,0:T(8,128)(2,1)} fusion(bf16[16,8,4096]{2,1,0:T(8,128)(2,1)S(1)} %all-to-all-done.2, f32[16,8]{0,1:T(8,128)S(1)} %bitcast.80, s32[16,8]{0,1:T(8,128)S(1)} %subtract_bitcast_fusion, pred[16,8]{0,1:T(8,128)(4,1)S(1)} %compare_bitcast_fusion), kind=kOutput, calls=%fused_computation.10 | convolution fusion | flops 50367488 | bytes 1115264 | tf_op jit(solution)/shard_map/emr,emd->rd/dot_general | solution.py:132
  (30 shorter events, 1.0 us)
Async XLA Ops:
  6.5 122.7 %copy-start = (bf16[16,4096]{1,0:T(8,128)(2,1)S(1)}, bf16[16,4096]{1,0:T(8,128)(2,1)}, u32[]{:S(2)}) copy-start(bf16[16,4096]{1,0:T(8,128)(2,1)} %param.19) | copy-start | bytes 393220
  6.5 11.3 %copy-start.5 = (s32[8]{0:T(128)S(1)}, s32[8]{0:T(128)}, u32[]{:S(2)}) copy-start(s32[8]{0:T(128)} %param.15) | copy-start | bytes 100
  6.5 11.3 %copy-start.3 = (bf16[8,2,512]{2,1,0:T(2,128)(2,1)S(1)}, bf16[8,2,512]{2,1,0:T(2,128)(2,1)}, u32[]{:S(2)}) copy-start(bf16[8,2,512]{2,1,0:T(2,128)(2,1)} %param.13) | copy-start | bytes 49156
  6.5 12.0 %copy-start.2 = (bf16[8,8192]{1,0:T(8,128)(2,1)S(1)}, bf16[8,8192]{1,0:T(8,128)(2,1)}, u32[]{:S(2)}) copy-start(bf16[8,8192]{1,0:T(8,128)(2,1)} %param.12) | copy-start | bytes 393220
  6.5 62.5 %all-gather.2.cloned.1.call-start = ((), (), s32[]{:S(2)}) async-start(), calls=%async_computation.3 | async-start | bytes 2228224 | tf_op jit(solution)/shard_map/all_gather | solution.py:74
  22.5 61.9 %copy-start.1 = (bf16[8,4096]{1,0:T(8,128)(2,1)S(1)}, bf16[8,4096]{1,0:T(8,128)(2,1)}, u32[]{:S(2)}) copy-start(bf16[8,4096]{1,0:T(8,128)(2,1)} %param.17) | copy-start | bytes 196612
  74.0 10.4 %all-to-all-start = ((bf16[16,8,256]{2,1,0:T(8,128)(2,1)}), bf16[16,8,256]{2,1,0:T(8,128)(2,1)S(1)}, u32[]{:S(2)}, u32[]{:S(2)}) async-start(bf16[16,8,256]{2,1,0:T(8,128)(2,1)} %fusion.21), calls=%async_computation | async-start | bytes 131072 | tf_op jit(solution)/shard_map/all_to_all | solution.py:79
  116.3 13.2 %copy-start.4 = (s32[8,8]{1,0:T(8,128)S(1)}, s32[8,8]{1,0:T(8,128)}, u32[]{:S(2)}) copy-start(s32[8,8]{1,0:T(8,128)} %param.20) | copy-start | bytes 772
  124.4 27.9 %all-to-all-start.2 = ((bf16[16,8,4096]{2,1,0:T(8,128)(2,1)}), bf16[16,8,4096]{2,1,0:T(8,128)(2,1)S(1)}, u32[]{:S(2)}, u32[]{:S(2)}) async-start(bf16[16,8,4096]{2,1,0:T(8,128)(2,1)} %fusion.9), calls=%async_computation.2 | async-start | bytes 2097152 | tf_op jit(solution)/shard_map/all_to_all | solution.py:122
Sparse Core Ops, SparseCore 0:
  24.9 44.0 all-gather.1
where the time goes:
time: 163 us; the launch traced here: 161 us
  waiting for transfers between devices  71.8 us (44%)
  blocking collectives  27.4 us (17%)
  matrix products  22.4 us (14%)
  between operations  13.6 us (8%)
  local copies, waits for them, and re-layouts  13.5 us (8%)
  starting transfers between devices  8.45 us (5%)
  other arithmetic  3.87 us (2%)
    all_gather x1, waiting for transfers between devices, per_device(): lax.all_gather(attended, 'pool', axis=0, tiled=True)  42.7 us
    all_to_all x1, blocking collectives, per_device(): lax.all_to_all(doubled, ('pool', 'sub'), split_axis=0, concat_axis=0, til...  27.4 us
    all_to_all x1, waiting for transfers between devices, per_device(): lax.all_to_all(half_out.reshape(-1, item_count, half_out.shape[-1]), ('po...  22.3 us
    dot_general x1, matrix products, per_device(): jnp.dot(inner_act, down_weight[0], preferred_element_type=jnp.float32)  8.06 us
    unnamed x16, local copies, waits for them, and re-layouts  6.9 us
    all_to_all x1, waiting for transfers between devices, per_device(): lax.all_to_all(partial_value.astype(jnp.bfloat16), ('pool', 'sub'), split...  6.74 us
    slice x1, local copies, waits for them, and re-layouts, attend(): cached_keys = kv_cache[:, :, 0].reshape(rows_att, cache_len, groups, HEAD)  6.55 us
    dot_general x1, matrix products, per_device(): lax.dot_general(lax.all_gather(attended, 'pool', axis=0, tiled=True), o_w...  4.99 us
  transfers between devices with their start and end apart: 3, of which 3 were waited for; matrix products, arithmetic and copies ran while one was open for 1% of the time, Pallas kernels for 0%

commit v1 on v0

--- a/solution.py
+++ b/solution.py
@@ -1,6 +1,10 @@
+import functools
+
 import jax
 import jax.numpy as jnp
 from jax import lax
+from jax.experimental import pallas as pl
+from jax.experimental.pallas import tpu as pltpu
 from jax.sharding import PartitionSpec as P
 
 QH = 64
@@ -133,6 +137,375 @@
     return mixed.astype(jnp.bfloat16)
 
 
+AG_CHUNKS = 2
+RS_CHUNKS = 4
+
+
+def contract(a, b, dims):
+    return lax.dot_general(a, b, ((dims[0], dims[1]), ((), ())), preferred_element_type=jnp.float32)
+
+
+def fold(value):
+    half = value.shape[1] // 2
+    return jnp.concatenate([value[:, :half], value[:, half:]], axis=0)
+
+
+def fused_kernel(
+    query, new_kv, kv, lengths, o_weight, residual, norm_gain, router, expert_ids, gate, up, down,
+    out,
+    kv_v, o_v, gate_v, up_v, down_v, q_s, att_s, gathered, small_out, small_in, hid, gate_acc, up_acc,
+    partial, sib_out, sib_in, x_out, x_in, z_out, z_in, own_sum,
+    load_sem, small_send, small_recv, ag_send, ag_recv, hid_send, hid_recv,
+    sib_send, sib_recv, x_send, x_recv, z_send, z_recv,
+):
+    me = lax.axis_index("pool")
+    core = lax.rem(me, 2)
+    x = lax.rem(me // 2, 2)
+    z = me // 4
+    sibling = z * 4 + x * 2 + (1 - core)
+    x_peer = z * 4 + (1 - x) * 2 + core
+
+    def z_of(j):
+        return lax.rem(z + j, 4)
+
+    def same_x(j):
+        return z_of(j) * 4 + x * 2 + core
+
+    def other_x(j):
+        return z_of(j) * 4 + (1 - x) * 2 + core
+
+    def flip(index):
+        return index - core + (1 - core)
+
+    def remote(src, dst, send_sem, recv_sem, target):
+        return pltpu.make_async_remote_copy(
+            src_ref=src, dst_ref=dst, send_sem=send_sem, recv_sem=recv_sem,
+            device_id={"pool": target}, device_id_type=pl.DeviceIdType.MESH,
+        )
+
+    barrier = pltpu.get_barrier_semaphore()
+    for offset in range(1, 16):
+        pl.semaphore_signal(
+            barrier, inc=1, device_id={"pool": lax.rem(me + offset, 16)},
+            device_id_type=pl.DeviceIdType.MESH,
+        )
+
+    loads = [pltpu.make_async_copy(kv.at[g], kv_v.at[g], load_sem.at[g]) for g in range(4)]
+    for at, (a, b) in enumerate(((o_weight, o_v), (gate, gate_v), (up, up_v), (down, down_v))):
+        loads.append(pltpu.make_async_copy(a, b, load_sem.at[4 + at]))
+    for load in loads:
+        load.start()
+
+    lane = lax.broadcasted_iota(jnp.int32, (8, 128), 1)
+    member = jnp.zeros((8, 128), jnp.float32)
+    for k in range(TOPK):
+        member = member + (expert_ids[:, k : k + 1] == lane).astype(jnp.float32)
+    member_pad = jnp.concatenate([member, jnp.zeros_like(member)], axis=0).astype(jnp.bfloat16)
+    res = residual[...].astype(jnp.float32)
+    for d in range(16):
+        small_out[d, 0:16, :] = fold(res[:, d * 256 : (d + 1) * 256]).astype(jnp.bfloat16)
+        small_out[d, 16:32, :] = member_pad
+    small_in[me] = small_out[me]
+
+    q_all = query[...].astype(jnp.float32)
+    for h in range(QH):
+        q_s[h] = q_all[:, h * 128 : (h + 1) * 128]
+
+    pl.semaphore_wait(barrier, 15)
+
+    def small_copy(offset):
+        target = lax.rem(me + offset, 16)
+        return remote(
+            small_out.at[target], small_in.at[me], small_send.at[offset], small_recv.at[me], target
+        )
+
+    def small_arrival(offset):
+        source = lax.rem(me + offset, 16)
+        return remote(
+            small_out.at[source], small_in.at[source], small_send.at[offset], small_recv.at[source], source
+        )
+
+    for offset in range(1, 16):
+        small_copy(offset).start()
+
+    score_scale = HEAD ** (-0.5)
+    position = lax.broadcasted_iota(jnp.int32, (16, 256), 1)
+    is_key = lax.rem(position, 2) == 0
+    position = position // 2
+
+    def attend_one(r, g, slot):
+        q_f = q_s[pl.ds(g * 16, 16), r, :]
+        both = kv_v[g, r]
+        scores = contract(q_f.astype(jnp.bfloat16), both, ((1,), (1,))) * score_scale
+        key = new_kv[r, g : g + 1, :]
+        value = new_kv[r, 4 + g : 5 + g, :]
+        own = jnp.sum(q_f * key, axis=1, keepdims=True) * score_scale
+        scores = jnp.where(is_key & (position < lengths[r]), scores, jnp.float32(-1e30))
+        top = jnp.maximum(jnp.max(scores, axis=1, keepdims=True), own)
+        weights = jnp.exp(scores - top)
+        own_weight = jnp.exp(own - top)
+        scale = 1.0 / (jnp.sum(weights, axis=1, keepdims=True) + own_weight)
+        probs = pltpu.roll(weights * scale, 1, 1).astype(jnp.bfloat16)
+        own_prob = (own_weight * scale).astype(jnp.bfloat16).astype(jnp.float32)
+        att_s[pl.ds(slot * 16, 16), r, :] = contract(probs, both, ((1,), (0,))) + own_prob * value
+
+    def gather_ops(buf, send_sem, recv_sem):
+        def send(source, target, n):
+            return remote(buf.at[source], buf.at[source], send_sem.at[n], recv_sem.at[source], target)
+
+        own = [send(me, same_x(j), j - 1) for j in (1, 2, 3)]
+        own += [send(me, x_peer, 3), send(me, sibling, 4)]
+
+        def arrive(source):
+            send(source, sibling, 0).wait_recv()
+
+        def relay_z(j):
+            arrive(same_x(j))
+            a = send(same_x(j), x_peer, 3 + 2 * j)
+            b = send(same_x(j), sibling, 4 + 2 * j)
+            a.start()
+            b.start()
+
+        def relay_x(j):
+            arrive(other_x(j))
+            send(other_x(j), sibling, 11 + j).start()
+
+        def finish():
+            for n in range(15):
+                send(me, sibling, n).wait_send()
+
+        return own, arrive, relay_z, relay_x, finish
+
+    rings = [
+        gather_ops(gathered.at[k], ag_send.at[k], ag_recv.at[k]) for k in range(AG_CHUNKS)
+    ]
+    for k in range(AG_CHUNKS):
+        for gg in range(2):
+            loads[2 * k + gg].wait()
+
+        def rows(step, carry, k=k):
+            for rr in range(4):
+                for gg in range(2):
+                    attend_one(step * 4 + rr, 2 * k + gg, gg)
+            return carry
+
+        lax.fori_loop(0, 2, rows, 0)
+        for h in range(16):
+            gathered[k, me, :, h * 128 : (h + 1) * 128] = jnp.concatenate(
+                [att_s[h], att_s[16 + h]], axis=0
+            ).astype(jnp.bfloat16)
+        for copy in rings[k][0]:
+            copy.start()
+
+    for k in range(AG_CHUNKS):
+        own, arrive, relay_z, relay_x, finish = rings[k]
+        for j in (1, 2, 3):
+            relay_z(j)
+        for j in (0, 1, 2, 3):
+            relay_x(j)
+    loads[4].wait()
+    total = jnp.zeros((128, 256), jnp.float32)
+    for k in range(AG_CHUNKS):
+        own, arrive, relay_z, relay_x, finish = rings[k]
+        for j in range(4):
+            arrive(flip(same_x(j)))
+            arrive(flip(other_x(j)))
+        left = gathered[k].reshape(256, 2048)
+        for gg in range(2):
+            first = k * 4096 + gg * 2048
+            product = contract(left, o_v[:, first : first + 2048], ((1,), (1,)))
+            total = total + product.reshape(16, 2, 8, 256)[:, gg].reshape(128, 256)
+
+    for offset in range(1, 16):
+        small_arrival(offset).wait_recv()
+    pieces = small_in[:, 0:16, :].astype(jnp.float32).reshape(16, 2, 8, 128)
+    res_part = jnp.concatenate(
+        [pieces[:, 0].reshape(128, 128), pieces[:, 1].reshape(128, 128)], axis=1
+    )
+    hid[me] = (total + res_part).astype(jnp.bfloat16)
+
+    own, arrive, relay_z, relay_x, finish_hid = gather_ops(hid, hid_send, hid_recv)
+    for copy in own:
+        copy.start()
+    loads[5].wait()
+    loads[6].wait()
+    for j in (1, 2, 3):
+        relay_z(j)
+
+    def project(pair, state, first=False):
+        square, logits = state
+        gate_sum = up_sum = None
+        for t in range(2):
+            s = pair * 2 + t
+            at = pl.ds(pl.multiple_of(s * 256, 256), 256)
+            h = hid[s].astype(jnp.float32)
+            square = square + jnp.sum(h * h, axis=1, keepdims=True)
+            scaled = (h * norm_gain[:, at].astype(jnp.float32)).astype(jnp.bfloat16)
+            logits = logits + contract(scaled, router[:, at], ((1,), (1,)))
+            a = contract(scaled, gate_v[at, :], ((1,), (0,)))
+            b = contract(scaled, up_v[at, :], ((1,), (0,)))
+            gate_sum = a if gate_sum is None else gate_sum + a
+            up_sum = b if up_sum is None else up_sum + b
+        if first:
+            gate_acc[...] = gate_sum
+            up_acc[...] = up_sum
+        else:
+            gate_acc[...] += gate_sum
+            up_acc[...] += up_sum
+        return square, logits
+
+    state = (jnp.zeros((128, 1), jnp.float32), jnp.zeros((128, 16), jnp.float32))
+    for j in range(4):
+        arrive(flip(same_x(j)))
+        state = project(z_of(j) * 2 + x, state, first=j == 0)
+        relay_x(j)
+    for j in range(4):
+        arrive(flip(other_x(j)))
+        state = project(z_of(j) * 2 + (1 - x), state)
+    square, logits = state
+    inv = lax.rsqrt(square * (1.0 / 4096) + norm_eps)
+    logits = logits * inv
+    members = small_in[:, 16:32, :].astype(jnp.float32)[:, 0:8, :].reshape(128, 128)[:, 0:16]
+    raised = jnp.where(members > 0.5, jnp.exp(logits), 0.0)
+    mine = lax.broadcasted_iota(jnp.int32, (128, 16), 1) == me
+    coef = jnp.sum(jnp.where(mine, raised, 0.0), axis=1, keepdims=True) / jnp.sum(
+        raised, axis=1, keepdims=True
+    )
+    gate_proj = gate_acc[...] * inv
+    inner = (gate_proj / (1.0 + jnp.exp(-gate_proj)) * (up_acc[...] * inv)).astype(jnp.bfloat16)
+    loads[7].wait()
+
+    width = 4096 // RS_CHUNKS
+
+    def sib_copy(n):
+        return remote(sib_out.at[n], sib_in.at[n], sib_send.at[n], sib_recv.at[n], sibling)
+
+    def x_copy(n):
+        return remote(x_out.at[n], x_in.at[n], x_send.at[n], x_recv.at[n], x_peer)
+
+    def z_copy(n, j):
+        return remote(
+            z_out.at[n, j - 1], z_in.at[n, j - 1], z_send.at[n, j - 1], z_recv.at[n, j - 1], same_x(j)
+        )
+
+    def stage_down(n):
+        product = contract(inner, down_v[:, n * width : (n + 1) * width], ((1,), (0,))) * coef
+        partial[n] = product.reshape(16, 8, width)
+        for chip in range(8):
+            sib_out[n, chip] = fold(partial[n, chip * 2 + (1 - core)]).astype(jnp.bfloat16)
+        sib_copy(n).start()
+
+    def chip_sum(n, chip):
+        return fold(partial[n, chip * 2 + core]) + sib_in[n, chip].astype(jnp.float32)
+
+    def stage_x(n):
+        sib_copy(n).wait_recv()
+        for zz in range(4):
+            x_out[n, zz] = chip_sum(n, zz * 2 + (1 - x)).astype(jnp.bfloat16)
+        x_copy(n).start()
+
+    def stage_z(n):
+        x_copy(n).wait_recv()
+        for j in range(4):
+            total = chip_sum(n, z_of(j) * 2 + x) + x_in[n, z_of(j)].astype(jnp.float32)
+            if j:
+                z_out[n, j - 1] = total.astype(jnp.bfloat16)
+                z_copy(n, j).start()
+            else:
+                own_sum[n] = total
+
+    def stage_end(n):
+        total = own_sum[n]
+        for j in (1, 2, 3):
+            z_copy(n, j).wait_recv()
+            total = total + z_in[n, j - 1].astype(jnp.float32)
+        out[:, n * width : (n + 1) * width] = jnp.concatenate(
+            [total[0:8], total[8:16]], axis=1
+        ).astype(jnp.bfloat16)
+
+    stages = (stage_down, stage_x, stage_z, stage_end)
+    for step in range(RS_CHUNKS + 3):
+        for depth, stage in enumerate(stages):
+            if 0 <= step - depth < RS_CHUNKS:
+                stage(step - depth)
+
+    for offset in range(1, 16):
+        small_copy(offset).wait_send()
+    for ring in rings:
+        ring[4]()
+    finish_hid()
+    for n in range(RS_CHUNKS):
+        sib_copy(n).wait_send()
+        x_copy(n).wait_send()
+        for j in (1, 2, 3):
+            z_copy(n, j).wait_send()
+
+
+def fused_device(
+    query, new_kv, kv_cache, lengths, o_weight, residual, norm_gain, router_weight, expert_ids,
+    gate_weight, up_weight, down_weight,
+):
+    bf16, f32 = jnp.bfloat16, jnp.float32
+    dma = pltpu.SemaphoreType.DMA
+    kv = kv_cache.reshape(8, 128, 2, 4, 128).transpose(3, 0, 1, 2, 4).reshape(4, 8, 256, 128)
+    new = new_kv.reshape(8, 8, 128).astype(f32)
+    half = 4096 // RS_CHUNKS // 2
+    vmem = pl.BlockSpec(memory_space=pltpu.VMEM)
+    smem = pl.BlockSpec(memory_space=pltpu.SMEM)
+    hbm = pl.BlockSpec(memory_space=pl.ANY)
+    return pl.pallas_call(
+        fused_kernel,
+        out_shape=jax.ShapeDtypeStruct((8, 4096), bf16),
+        in_specs=[vmem, vmem, hbm, smem, hbm, vmem, vmem, vmem, vmem, hbm, hbm, hbm],
+        out_specs=vmem,
+        scratch_shapes=[
+            pltpu.VMEM((4, 8, 256, 128), bf16),
+            pltpu.VMEM((256, 8192), bf16),
+            pltpu.VMEM((4096, 768), bf16),
+            pltpu.VMEM((4096, 768), bf16),
+            pltpu.VMEM((768, 4096), bf16),
+            pltpu.VMEM((64, 8, 128), f32),
+            pltpu.VMEM((32, 8, 128), f32),
+            pltpu.VMEM((AG_CHUNKS, 16, 16, 2048), bf16),
+            pltpu.VMEM((16, 32, 128), bf16),
+            pltpu.VMEM((16, 32, 128), bf16),
+            pltpu.VMEM((16, 128, 256), bf16),
+            pltpu.VMEM((128, 768), f32),
+            pltpu.VMEM((128, 768), f32),
+            pltpu.VMEM((RS_CHUNKS, 16, 8, 2 * half), f32),
+            pltpu.VMEM((RS_CHUNKS, 8, 16, half), bf16),
+            pltpu.VMEM((RS_CHUNKS, 8, 16, half), bf16),
+            pltpu.VMEM((RS_CHUNKS, 4, 16, half), bf16),
+            pltpu.VMEM((RS_CHUNKS, 4, 16, half), bf16),
+            pltpu.VMEM((RS_CHUNKS, 3, 16, half), bf16),
+            pltpu.VMEM((RS_CHUNKS, 3, 16, half), bf16),
+            pltpu.VMEM((RS_CHUNKS, 16, half), f32),
+            dma((8,)),
+            dma((16,)),
+            dma((16,)),
+            dma((AG_CHUNKS, 15)),
+            dma((AG_CHUNKS, 16)),
+            dma((15,)),
+            dma((16,)),
+            dma((RS_CHUNKS,)),
+            dma((RS_CHUNKS,)),
+            dma((RS_CHUNKS,)),
+            dma((RS_CHUNKS,)),
+            dma((RS_CHUNKS, 3)),
+            dma((RS_CHUNKS, 3)),
+        ],
+        compiler_params=pltpu.CompilerParams(
+            collective_id=0, has_side_effects=True, vmem_limit_bytes=56 * 1024 * 1024
+        ),
+        cost_estimate=pl.CostEstimate(
+            flops=3_500_000_000, bytes_accessed=27_000_000, transcendentals=300_000
+        ),
+    )(
+        query, new, kv, lengths, o_weight, residual, norm_gain.reshape(1, 4096), router_weight,
+        expert_ids, gate_weight[0], up_weight[0], down_weight[0],
+    )
+
+
 def solution(mesh):
     in_specs = (
         P(("groups", "pool"), "sub"),
@@ -149,6 +522,8 @@
         P("pool", "sub", None),
     )
     out_specs = P(("groups", "pool", "sub"), None)
+    sizes = dict(mesh.shape)
+    fused = sizes["pool"] == 16 and sizes["sub"] == 1
     return jax.shard_map(
-        per_device, mesh=mesh, in_specs=in_specs, out_specs=out_specs, check_vma=False
-    )
+        fused_device if fused else per_device, mesh=mesh, in_specs=in_specs, out_specs=out_specs, check_vma=False
+    )

time: 163 us -> 76.1 us (0.47)
  waiting for transfers between devices: 71.8 us -> 0 us
  Pallas kernels: 0 us -> 67.9 us
  blocking collectives: 27.4 us -> 0 us
  matrix products: 22.4 us -> 0 us
  between operations: 13.6 us -> 0.01 us
  starting transfers between devices: 8.45 us -> 0 us
  local copies, waits for them, and re-layouts: 13.5 us -> 7.84 us
  other arithmetic: 3.87 us -> 0 us
    pallas_call x0 -> x1, Pallas kernels: none -> 67.9 us  [fused_device(): pl.pallas_call(fused_kernel, out_shape=jax.ShapeDtypeStruct((8, 4096), bf...]
    all_gather x1 -> x0, waiting for transfers between devices: 42.7 us -> none  [per_device(): lax.all_gather(attended, 'pool', axis=0, tiled=True)]
    all_to_all x2 -> x0, waiting for transfers between devices: 29.1 us -> none  [the longest x1 22.3 us: per_device(): lax.all_to_all(half_out.reshape(-1, item_count, half_out.shape[-1]), ('po...]
    all_to_all x1 -> x0, blocking collectives: 27.4 us -> none  [per_device(): lax.all_to_all(doubled, ('pool', 'sub'), split_axis=0, concat_axis=0, til...]
    dot_general x9 -> x0, matrix products: 22.4 us -> none  [the longest x1 8.06 us: per_device(): jnp.dot(inner_act, down_weight[0], preferred_element_type=jnp.float32)]
    all_to_all x2 -> x0, starting transfers between devices: 8.42 us -> none  [the longest x1 4.92 us: per_device(): lax.all_to_all(half_out.reshape(-1, item_count, half_out.shape[-1]), ('po...]
    slice x1 -> x0, local copies, waits for them, and re-layouts: 6.55 us -> none  [attend(): cached_keys = kv_cache[:, :, 0].reshape(rows_att, cache_len, groups, HEAD)]
    unnamed x16 -> x3, local copies, waits for them, and re-layouts: 6.9 us -> 1.48 us
  transfers between devices with their start and end apart: 3 -> 0, of which waited for: 3 -> 0; matrix products, arithmetic and copies ran while one was open for 1% -> 0% of each run, Pallas kernels for 0% -> 0%
where the time goes in v1:
time: 76.1 us; the launch traced here: 75.8 us
  Pallas kernels  67.9 us (89%)
  local copies, waits for them, and re-layouts  7.84 us (10%)
    pallas_call x1, Pallas kernels, fused_device(): pl.pallas_call(fused_kernel, out_shape=jax.ShapeDtypeStruct((8, 4096), bf...  67.9 us
    reshape x1, local copies, waits for them, and re-layouts, fused_device(): kv_cache.reshape(8, 128, 2, 4, 128).transpose(3, 0, 1, 2, 4)  3.57 us

profile of v1, /device:TPU:0, one launch (start us, length us, event | category | flops | bytes accessed | tf_op | source)
XLA Modules:
  0.0 75.8 jit_solution(9362810333186691083)
XLA Ops:
  0.0 0.0 copy-start
  0.0 1.5 %reshape.14.norm_gain = bf16[1,4096]{1,0:T(2,128)(2,1)} reshape(bf16[4096]{0:T(1024)(128)(2,1)} %param.18) | data formatting | bytes 16384 | tf_op jit(solution)/shard_map/reshape | solution.py:504
  1.5 1.3 %reshape.15.new_kv = f32[8,8,128]{2,1,0:T(8,128)} reshape(bf16[8,2,512]{2,1,0:T(2,128)(2,1)} %param.13) | data formatting | bytes 49152 | tf_op jit(solution)/shard_map/convert_element_type | solution.py:451
  2.8 0.0 copy-done
  2.8 3.6 %copy_bitcast_fusion = bf16[8,128,2,4,128]{4,2,1,0,3:T(2,128)(2,1)} fusion(bf16[8,128,2,512]{3,2,1,0:T(2,128)(2,1)S(1)} %copy-done), kind=kLoop, calls=%fused_computation | loop fusion | bytes 4194304 | tf_op jit(solution)/shard_map/reshape | solution.py:450
  6.4 67.9 %shard_map.118 = bf16[8,4096]{1,0:T(8,128)(2,1)} custom-call(bf16[8,8192]{1,0:T(8,128)(2,1)} %query.1, f32[8,8,128]{2,1,0:T(8,128)} %reshape.15.new_kv, bf16[4,8,256,128]{3,2,1,0:T(8,128)(2,1)} %bitcast.11, s32[8]{0:T(128)} %lengths.1, bf16[256,8192]{1,0:T(8,128)(2,1)} %o_weight.1, bf16[8,4096]{1,0:T(8,128)(2,1)} %residual.1, ...), custom_call_target="tpu_custom_call" | custom-call | flops 3500000000 | bytes 27000000 | tf_op jit(solution)/shard_map/pallas_call | solution.py:456
  74.3 1.5 %copy.17 = bf16[8,4096]{1,0:T(8,128)(2,1)} copy(bf16[8,4096]{1,0:T(8,128)(2,1)} %shard_map.118) | data formatting | bytes 131072
Async XLA Ops:
  0.0 2.8 %copy-start = (bf16[8,128,2,512]{3,2,1,0:T(2,128)(2,1)S(1)}, bf16[8,128,2,512]{3,2,1,0:T(2,128)(2,1)}, u32[]{:S(2)}) copy-start(bf16[8,128,2,512]{3,2,1,0:T(2,128)(2,1)} %param.14) | copy-start | bytes 6291460

commit v2 on v1

--- a/solution.py
+++ b/solution.py
@@ -139,6 +139,8 @@
 
 AG_CHUNKS = 2
 RS_CHUNKS = 4
+HID_CHUNKS = 2
+hid_rows = 128 // HID_CHUNKS
 
 
 def contract(a, b, dims):
@@ -155,7 +157,7 @@
     out,
     kv_v, o_v, gate_v, up_v, down_v, q_s, att_s, gathered, small_out, small_in, hid, gate_acc, up_acc,
     partial, sib_out, sib_in, x_out, x_in, z_out, z_in, own_sum,
-    load_sem, small_send, small_recv, ag_send, ag_recv, hid_send, hid_recv,
+    gain_row, load_sem, small_send, small_recv, ag_send, ag_recv, hid_send, hid_recv,
     sib_send, sib_recv, x_send, x_recv, z_send, z_recv,
 ):
     me = lax.axis_index("pool")
@@ -190,10 +192,13 @@
             device_id_type=pl.DeviceIdType.MESH,
         )
 
-    loads = [pltpu.make_async_copy(kv.at[g], kv_v.at[g], load_sem.at[g]) for g in range(4)]
+    loads = [
+        pltpu.make_async_copy(kv.at[:, :, :, pl.ds(g * 128, 128)], kv_v.at[g], load_sem.at[g])
+        for g in range(4)
+    ]
     for at, (a, b) in enumerate(((o_weight, o_v), (gate, gate_v), (up, up_v), (down, down_v))):
         loads.append(pltpu.make_async_copy(a, b, load_sem.at[4 + at]))
-    for load in loads:
+    for load in loads[:4]:
         load.start()
 
     lane = lax.broadcasted_iota(jnp.int32, (8, 128), 1)
@@ -228,26 +233,39 @@
     for offset in range(1, 16):
         small_copy(offset).start()
 
+    kv_rows = kv_v.reshape(4, 8, 256, 128)
     score_scale = HEAD ** (-0.5)
     position = lax.broadcasted_iota(jnp.int32, (16, 256), 1)
     is_key = lax.rem(position, 2) == 0
     position = position // 2
 
-    def attend_one(r, g, slot):
-        q_f = q_s[pl.ds(g * 16, 16), r, :]
-        both = kv_v[g, r]
-        scores = contract(q_f.astype(jnp.bfloat16), both, ((1,), (1,))) * score_scale
-        key = new_kv[r, g : g + 1, :]
-        value = new_kv[r, 4 + g : 5 + g, :]
-        own = jnp.sum(q_f * key, axis=1, keepdims=True) * score_scale
-        scores = jnp.where(is_key & (position < lengths[r]), scores, jnp.float32(-1e30))
+    def attend_group(g, slot):
+        queries = [q_s[pl.ds(g * 16, 16), r, :] for r in range(8)]
+        fresh = [new_kv[r, :, g * 128 : (g + 1) * 128].astype(jnp.float32) for r in range(8)]
+        scores = [
+            jnp.where(
+                is_key & (position < lengths[r]),
+                contract(queries[r].astype(jnp.bfloat16), kv_rows[g, r], ((1,), (1,))) * score_scale,
+                jnp.float32(-1e30),
+            )
+            for r in range(8)
+        ]
+        scores = jnp.concatenate(scores, axis=0)
+        keys = jnp.concatenate([jnp.broadcast_to(f[0:1], (16, 128)) for f in fresh], axis=0)
+        own = jnp.sum(jnp.concatenate(queries, axis=0) * keys, axis=1, keepdims=True) * score_scale
         top = jnp.maximum(jnp.max(scores, axis=1, keepdims=True), own)
         weights = jnp.exp(scores - top)
         own_weight = jnp.exp(own - top)
         scale = 1.0 / (jnp.sum(weights, axis=1, keepdims=True) + own_weight)
         probs = pltpu.roll(weights * scale, 1, 1).astype(jnp.bfloat16)
         own_prob = (own_weight * scale).astype(jnp.bfloat16).astype(jnp.float32)
-        att_s[pl.ds(slot * 16, 16), r, :] = contract(probs, both, ((1,), (0,))) + own_prob * value
+        results = [
+            contract(probs[r * 16 : (r + 1) * 16], kv_rows[g, r], ((1,), (0,)))
+            + own_prob[r * 16 : (r + 1) * 16] * fresh[r][1:2]
+            for r in range(8)
+        ]
+        for r in range(8):
+            att_s[pl.ds(slot * 16, 16), r, :] = results[r]
 
     def gather_ops(buf, send_sem, recv_sem):
         def send(source, target, n):
@@ -282,14 +300,11 @@
     for k in range(AG_CHUNKS):
         for gg in range(2):
             loads[2 * k + gg].wait()
-
-        def rows(step, carry, k=k):
-            for rr in range(4):
-                for gg in range(2):
-                    attend_one(step * 4 + rr, 2 * k + gg, gg)
-            return carry
-
-        lax.fori_loop(0, 2, rows, 0)
+        if k == 0:
+            for load in loads[4:]:
+                load.start()
+        for gg in range(2):
+            attend_group(2 * k + gg, gg)
         for h in range(16):
             gathered[k, me, :, h * 128 : (h + 1) * 128] = jnp.concatenate(
                 [att_s[h], att_s[16 + h]], axis=0
@@ -297,12 +312,12 @@
         for copy in rings[k][0]:
             copy.start()
 
-    for k in range(AG_CHUNKS):
-        own, arrive, relay_z, relay_x, finish = rings[k]
+    for ring in rings:
         for j in (1, 2, 3):
-            relay_z(j)
+            ring[2](j)
+    for ring in rings:
         for j in (0, 1, 2, 3):
-            relay_x(j)
+            ring[3](j)
     loads[4].wait()
     total = jnp.zeros((128, 256), jnp.float32)
     for k in range(AG_CHUNKS):
@@ -322,15 +337,18 @@
     res_part = jnp.concatenate(
         [pieces[:, 0].reshape(128, 128), pieces[:, 1].reshape(128, 128)], axis=1
     )
-    hid[me] = (total + res_part).astype(jnp.bfloat16)
-
-    own, arrive, relay_z, relay_x, finish_hid = gather_ops(hid, hid_send, hid_recv)
-    for copy in own:
-        copy.start()
+    gain_row[...] = norm_gain[...].reshape(1, 4096).astype(jnp.float32)
+    hidden = (total + res_part).astype(jnp.bfloat16)
+    hid_rings = [gather_ops(hid.at[k], hid_send.at[k], hid_recv.at[k]) for k in range(HID_CHUNKS)]
+    for k in range(HID_CHUNKS):
+        hid[k, me] = hidden[k * hid_rows : (k + 1) * hid_rows]
+        for copy in hid_rings[k][0]:
+            copy.start()
     loads[5].wait()
     loads[6].wait()
-    for j in (1, 2, 3):
-        relay_z(j)
+    for ring in hid_rings:
+        for j in (1, 2, 3):
+            ring[2](j)
 
     def project(pair, state, first=False):
         square, logits = state
@@ -338,9 +356,9 @@
         for t in range(2):
             s = pair * 2 + t
             at = pl.ds(pl.multiple_of(s * 256, 256), 256)
-            h = hid[s].astype(jnp.float32)
+            h = jnp.concatenate([hid[k, s] for k in range(HID_CHUNKS)], axis=0).astype(jnp.float32)
             square = square + jnp.sum(h * h, axis=1, keepdims=True)
-            scaled = (h * norm_gain[:, at].astype(jnp.float32)).astype(jnp.bfloat16)
+            scaled = (h * gain_row[:, at]).astype(jnp.bfloat16)
             logits = logits + contract(scaled, router[:, at], ((1,), (1,)))
             a = contract(scaled, gate_v[at, :], ((1,), (0,)))
             b = contract(scaled, up_v[at, :], ((1,), (0,)))
@@ -356,11 +374,14 @@
 
     state = (jnp.zeros((128, 1), jnp.float32), jnp.zeros((128, 16), jnp.float32))
     for j in range(4):
-        arrive(flip(same_x(j)))
+        for ring in hid_rings:
+            ring[1](flip(same_x(j)))
         state = project(z_of(j) * 2 + x, state, first=j == 0)
-        relay_x(j)
+        for ring in hid_rings:
+            ring[3](j)
     for j in range(4):
-        arrive(flip(other_x(j)))
+        for ring in hid_rings:
+            ring[1](flip(other_x(j)))
         state = project(z_of(j) * 2 + (1 - x), state)
     square, logits = state
     inv = lax.rsqrt(square * (1.0 / 4096) + norm_eps)
@@ -423,17 +444,16 @@
             [total[0:8], total[8:16]], axis=1
         ).astype(jnp.bfloat16)
 
-    stages = (stage_down, stage_x, stage_z, stage_end)
-    for step in range(RS_CHUNKS + 3):
-        for depth, stage in enumerate(stages):
-            if 0 <= step - depth < RS_CHUNKS:
-                stage(step - depth)
+    for stage in (stage_down, stage_x, stage_z, stage_end):
+        for n in range(RS_CHUNKS):
+            stage(n)
 
     for offset in range(1, 16):
         small_copy(offset).wait_send()
     for ring in rings:
         ring[4]()
-    finish_hid()
+    for ring in hid_rings:
+        ring[4]()
     for n in range(RS_CHUNKS):
         sib_copy(n).wait_send()
         x_copy(n).wait_send()
@@ -447,8 +467,6 @@
 ):
     bf16, f32 = jnp.bfloat16, jnp.float32
     dma = pltpu.SemaphoreType.DMA
-    kv = kv_cache.reshape(8, 128, 2, 4, 128).transpose(3, 0, 1, 2, 4).reshape(4, 8, 256, 128)
-    new = new_kv.reshape(8, 8, 128).astype(f32)
     half = 4096 // RS_CHUNKS // 2
     vmem = pl.BlockSpec(memory_space=pltpu.VMEM)
     smem = pl.BlockSpec(memory_space=pltpu.SMEM)
@@ -459,7 +477,7 @@
         in_specs=[vmem, vmem, hbm, smem, hbm, vmem, vmem, vmem, vmem, hbm, hbm, hbm],
         out_specs=vmem,
         scratch_shapes=[
-            pltpu.VMEM((4, 8, 256, 128), bf16),
+            pltpu.VMEM((4, 8, 128, 2, 128), bf16),
             pltpu.VMEM((256, 8192), bf16),
             pltpu.VMEM((4096, 768), bf16),
             pltpu.VMEM((4096, 768), bf16),
@@ -469,7 +487,7 @@
             pltpu.VMEM((AG_CHUNKS, 16, 16, 2048), bf16),
             pltpu.VMEM((16, 32, 128), bf16),
             pltpu.VMEM((16, 32, 128), bf16),
-            pltpu.VMEM((16, 128, 256), bf16),
+            pltpu.VMEM((HID_CHUNKS, 16, hid_rows, 256), bf16),
             pltpu.VMEM((128, 768), f32),
             pltpu.VMEM((128, 768), f32),
             pltpu.VMEM((RS_CHUNKS, 16, 8, 2 * half), f32),
@@ -480,13 +498,14 @@
             pltpu.VMEM((RS_CHUNKS, 3, 16, half), bf16),
             pltpu.VMEM((RS_CHUNKS, 3, 16, half), bf16),
             pltpu.VMEM((RS_CHUNKS, 16, half), f32),
+            pltpu.VMEM((1, 4096), f32),
             dma((8,)),
             dma((16,)),
             dma((16,)),
             dma((AG_CHUNKS, 15)),
             dma((AG_CHUNKS, 16)),
-            dma((15,)),
-            dma((16,)),
+            dma((HID_CHUNKS, 15)),
+            dma((HID_CHUNKS, 16)),
             dma((RS_CHUNKS,)),
             dma((RS_CHUNKS,)),
             dma((RS_CHUNKS,)),
@@ -501,7 +520,7 @@
             flops=3_500_000_000, bytes_accessed=27_000_000, transcendentals=300_000
         ),
     )(
-        query, new, kv, lengths, o_weight, residual, norm_gain.reshape(1, 4096), router_weight,
+        query, new_kv, kv_cache, lengths, o_weight, residual, norm_gain, router_weight,
         expert_ids, gate_weight[0], up_weight[0], down_weight[0],
     )
 

time: 76.1 us -> 62.5 us (0.82)
  Pallas kernels: 67.9 us -> 60.9 us
  local copies, waits for them, and re-layouts: 7.84 us -> 1.47 us
    pallas_call x1, Pallas kernels: 67.9 us -> 60.9 us  [fused_device(): pl.pallas_call(fused_kernel, out_shape=jax.ShapeDtypeStruct((8, 4096), bf...]
    reshape x2 -> x0, local copies, waits for them, and re-layouts: 5.02 us -> none  [the longest x1 3.57 us: fused_device(): kv_cache.reshape(8, 128, 2, 4, 128).transpose(3, 0, 1, 2, 4)]
    convert_element_type x1 -> x0, local copies, waits for them, and re-layouts: 1.34 us -> none  [fused_device(): new = new_kv.reshape(8, 8, 128).astype(f32)]
where the time goes in v2:
time: 62.5 us; the launch traced here: 62.3 us
  Pallas kernels  60.9 us (97%)
  local copies, waits for them, and re-layouts  1.47 us (2%)
    pallas_call x1, Pallas kernels, fused_device(): pl.pallas_call(fused_kernel, out_shape=jax.ShapeDtypeStruct((8, 4096), bf...  60.9 us
    unnamed x1, local copies, waits for them, and re-layouts  1.47 us

profile of v2, /device:TPU:0, one launch (start us, length us, event | category | flops | bytes accessed | tf_op | source)
XLA Modules:
  0.0 62.3 jit_solution(17259532105156275275)
XLA Ops:
  0.0 60.9 %shard_map.118 = bf16[8,4096]{1,0:T(8,128)(2,1)} custom-call(bf16[8,8192]{1,0:T(8,128)(2,1)} %query.1, bf16[8,2,512]{2,1,0:T(2,128)(2,1)} %new_kv.1, bf16[8,128,2,512]{3,2,1,0:T(2,128)(2,1)} %kv.1, s32[8]{0:T(128)} %lengths.1, bf16[256,8192]{1,0:T(8,128)(2,1)} %o_weight.1, bf16[8,4096]{1,0:T(8,128)(2,1)} %residual.1, bf16[4096]{0:T(1024)(128)(2,1)} %norm_gain.1, ...), custom_call_target="tpu_custom_call" | custom-call | flops 3500000000 | bytes 27000000 | tf_op jit(solution)/shard_map/pallas_call | solution.py:474
  60.9 1.5 %copy.14 = bf16[8,4096]{1,0:T(8,128)(2,1)} copy(bf16[8,4096]{1,0:T(8,128)(2,1)} %shard_map.118) | data formatting | bytes 131072

commit v3 on v2

--- a/solution.py
+++ b/solution.py
@@ -168,7 +168,7 @@
     x_peer = z * 4 + (1 - x) * 2 + core
 
     def z_of(j):
-        return lax.rem(z + j, 4)
+        return (z, z + 1 - 2 * lax.rem(z, 2), z + 2 - 4 * (z // 2), 3 - z)[j]
 
     def same_x(j):
         return z_of(j) * 4 + x * 2 + core
@@ -216,8 +216,6 @@
     for h in range(QH):
         q_s[h] = q_all[:, h * 128 : (h + 1) * 128]
 
-    pl.semaphore_wait(barrier, 15)
-
     def small_copy(offset):
         target = lax.rem(me + offset, 16)
         return remote(
@@ -229,9 +227,6 @@
         return remote(
             small_out.at[source], small_in.at[source], small_send.at[offset], small_recv.at[source], source
         )
-
-    for offset in range(1, 16):
-        small_copy(offset).start()
 
     kv_rows = kv_v.reshape(4, 8, 256, 128)
     score_scale = HEAD ** (-0.5)
@@ -309,8 +304,13 @@
             gathered[k, me, :, h * 128 : (h + 1) * 128] = jnp.concatenate(
                 [att_s[h], att_s[16 + h]], axis=0
             ).astype(jnp.bfloat16)
+        if k == 0:
+            pl.semaphore_wait(barrier, 15)
         for copy in rings[k][0]:
             copy.start()
+        if k == 0:
+            for offset in range(1, 16):
+                small_copy(offset).start()
 
     for ring in rings:
         for j in (1, 2, 3):

time: 62.5 us -> 59.4 us (0.950)
  Pallas kernels: 60.9 us -> 57.7 us
    pallas_call x1, Pallas kernels: 60.9 us -> 57.7 us  [fused_device(): pl.pallas_call(fused_kernel, out_shape=jax.ShapeDtypeStruct((8, 4096), bf...]
where the time goes in v3:
time: 59.4 us; the launch traced here: 59.2 us
  Pallas kernels  57.7 us (97%)
  local copies, waits for them, and re-layouts  1.47 us (2%)
    pallas_call x1, Pallas kernels, fused_device(): pl.pallas_call(fused_kernel, out_shape=jax.ShapeDtypeStruct((8, 4096), bf...  57.7 us
    unnamed x1, local copies, waits for them, and re-layouts  1.47 us

profile of v3, /device:TPU:0, one launch (start us, length us, event | category | flops | bytes accessed | tf_op | source)
XLA Modules:
  0.0 59.2 jit_solution(16247117159393493737)
XLA Ops:
  0.0 57.7 %shard_map.118 = bf16[8,4096]{1,0:T(8,128)(2,1)} custom-call(bf16[8,8192]{1,0:T(8,128)(2,1)} %query.1, bf16[8,2,512]{2,1,0:T(2,128)(2,1)} %new_kv.1, bf16[8,128,2,512]{3,2,1,0:T(2,128)(2,1)} %kv.1, s32[8]{0:T(128)} %lengths.1, bf16[256,8192]{1,0:T(8,128)(2,1)} %o_weight.1, bf16[8,4096]{1,0:T(8,128)(2,1)} %residual.1, bf16[4096]{0:T(1024)(128)(2,1)} %norm_gain.1, ...), custom_call_target="tpu_custom_call" | custom-call | flops 3500000000 | bytes 27000000 | tf_op jit(solution)/shard_map/pallas_call | solution.py:474
  57.7 1.5 %copy.14 = bf16[8,4096]{1,0:T(8,128)(2,1)} copy(bf16[8,4096]{1,0:T(8,128)(2,1)} %shard_map.118) | data formatting | bytes 131072
